TPU v7x, 32 devices: a whole 2x2x4 slice. The times are simulated.
32 devices in a mesh: group: 2 (over x), node: 16 (over z, y, core).
Axes of the slice: x: 2, y: 2, z: 4, core: 2. Of those that a mesh axis runs over, the one named last changes fastest.
Arguments:
- right_side: float32 [120, 12288], P(None, ('group', 'node')), parts along dimension 1, may hold values from -130 to 130
- initial: float32 [120, 12288], P(None, ('group', 'node')), parts along dimension 1, may hold values from -3 to 3
- galerkin_mats: float32 [10, 120, 120], replicated, may hold values from -0.1 to 2.5, as said below
- stiffness_tiles: float32 [10, 96, 4, 128, 128], P(None, ('group', 'node')), parts along dimension 1, may hold values from -0.004 to 0.235, as said below
- block_cols: int32 [96, 4], P(('group', 'node')), parts along dimension 0, may hold values from 0 to 47, as said below
Outputs:
- solution_field: float32 [120, 12288], P(None, ('group', 'node')), parts along dimension 1
- residual: float32 [120, 12288], P(None, ('group', 'node')), parts along dimension 1
There are 2 independent parts, one for each index of `group`. A program takes and returns all parts, laid end to end along the dimension named above; an argument that names none is the same for every part. Nothing has to cross between parts.
Inputs may be any that keep to these rules, and one draw needn't show every extreme that they name: `galerkin_mats`: each G_k is symmetric. `stiffness_tiles`: each K_k is symmetric: the tile of block row b at block column c is the transpose of the tile of row c at column b; where b has no block b-1 or b+1, that slot names b and holds zeros. `block_cols`: block row b names b, b-1 and b+1 where they exist (else b again), and one partner block at distance 2 or 3 inside its aligned group of 6 blocks, the partner of that block being b; the order of the slots is arbitrary for each row.
All inputs are finite; a program needn't handle non-finite values.
Results may differ from a plain program's by a relative error of at most 0.0003.
Values sent between devices are 32-bit elements; how exact they have to be, the bound alone decides.
A program may use at most 64 MiB of HBM per device.

v0:
```python
import jax
import jax.numpy as jnp
from jax import lax
from jax.sharding import PartitionSpec as P

ITERS = 2


def extended(block, sides, width):
    for axis, dim in sides:
        count = lax.axis_size(axis)
        forward = [(i, i + 1) for i in range(count - 1)]
        backward = [(target, source) for source, target in forward]
        low = lax.ppermute(
            lax.slice_in_dim(block, block.shape[dim] - width, None, axis=dim), axis, forward
        )
        high = lax.ppermute(lax.slice_in_dim(block, 0, width, axis=dim), axis, backward)
        block = jnp.concatenate([low, block, high], axis=dim)
    return block


def build_window(values_in, block_width, block_count):
    coef_count = values_in.shape[0]
    padded = extended(values_in, (("node", 1),), 3 * block_width)
    return padded.reshape(coef_count, block_count + 6, block_width)


def apply_field(values_in, stiffness_tiles, block_cols, galerkin_mats):
    block_width = stiffness_tiles.shape[-1]
    block_count = block_cols.shape[0]
    blocks = build_window(values_in, block_width, block_count)
    offset = lax.axis_index("node") * block_count
    local_index = block_cols - offset + 3
    picked = jnp.take(blocks, local_index, axis=1)
    mixed_terms = jnp.einsum(
        "kbsij,pbsj->kpbi", stiffness_tiles, picked, precision=lax.Precision.HIGHEST
    )
    result = jnp.einsum(
        "kpq,kqbi->pbi", galerkin_mats, mixed_terms, precision=lax.Precision.HIGHEST
    )
    return result.reshape(values_in.shape)


def squares(residual):
    return lax.psum(jnp.sum(residual * residual), "node")


def per_device(right_side, initial, galerkin_mats, stiffness_tiles, block_cols):

    def operate(vector):
        return apply_field(vector, stiffness_tiles, block_cols, galerkin_mats)

    solution_field = initial
    residual = right_side - operate(initial)
    direction = residual
    norm_now = squares(residual)
    for iteration in range(ITERS):
        applied = operate(direction)
        step_length = norm_now / lax.psum(jnp.sum(direction * applied), "node")
        solution_field = solution_field + step_length * direction
        residual = residual - step_length * applied
        norm_next = squares(residual)
        direction = residual + norm_next / norm_now * direction
        norm_now = norm_next
    return (solution_field, residual)


def solution(mesh):
    placed = (
        P(None, ("group", "node")),
        P(None, ("group", "node")),
        P(),
        P(None, ("group", "node"), None, None, None),
        P(("group", "node"), None),
    )
    return jax.shard_map(
        per_device,
        mesh=mesh,
        in_specs=placed,
        out_specs=(P(None, ("group", "node")), P(None, ("group", "node"))),
        check_vma=False,
    )
```

profile of v0, /device:TPU:0, one launch (start us, length us, event | category | flops | bytes accessed | tf_op | source)
XLA Modules:
  0.0 169.1 jit_solution(11282070768447876286)
XLA Ops:
  0.6 2.5 %collective-permute-start = (f32[120,384]{1,0:T(8,128)}, f32[120,384]{1,0:T(8,128)S(1)}, u32[]{:S(2)}, u32[]{:S(2)}) collective-permute-start(f32[120,384]{1,0:T(8,128)} %param.8), channel_id=1, source_target_pairs={{0,1},{1,2},{2,3},{3,4},{4,5},{5,6},{6,7},{7,8},{8,9},{9,10},{10,1... | collective-permute-start | bytes 552968 | tf_op jit(solution)/shard_map/ppermute | solution.py:14
  3.2 1.3 collective-permute-start.1
  4.5 0.7 compare_and_fusion
  5.2 1.0 copy.10
  6.3 2.5 %collective-permute-done.1 = f32[120,384]{1,0:T(8,128)S(1)} collective-permute-done((f32[120,384]{1,0:T(8,128)}, f32[120,384]{1,0:T(8,128)S(1)}, u32[]{:S(2)}, u32[]{:S(2)}) %collective-permute-start.1) | collective-permute-done | bytes 184352 | tf_op jit(solution)/shard_map/ppermute | solution.py:17
  8.8 1.0 pad_maximum_fusion.2
  9.8 0.2 copy.7
  10.0 0.2 copy.8
  10.2 0.6 gather_fusion
  10.9 10.1 %fusion.4 = f32[3,120,10,128,1]{3,1,4,2,0:T(8,128)S(1)} fusion(f32[10,3,4,128,128]{4,3,2,1,0:T(8,128)} %param.10, f32[3,4,120,128]{3,2,1,0:T(8,128)S(1)} %bitcast.96, pred[3,4]{1,0:T(4,128)(4,1)S(1)} %get-tuple-element.9), kind=kOutput, calls=%fused_computation.7 | convolution fusion | flops 2831339520 | bytes 10444812 | tf_op jit(solution)/shard_map/kbsij,pbsj->kpbi/dot_general | solution.py:35
  21.0 1.6 fusion.12
  22.8 6.0 %collective-permute-start.2 = (f32[120,384]{0,1:T(8,128)S(1)}, f32[120,384]{0,1:T(8,128)S(1)}, u32[]{:S(2)}, u32[]{:S(2)}) collective-permute-start(f32[120,384]{0,1:T(8,128)S(1)} %bitcast_subtract_fusion), channel_id=1, source_target_pairs={{0,1},{1,2},{2,3},{3,4},{4,5},{5,6},{6,7},{7,8},{8,9},{9,10},{10,1... | collective-permute-start | bytes 552968 | tf_op jit(solution)/shard_map/ppermute | solution.py:14
  28.8 1.3 collective-permute-start.3
  30.1 2.0 %collective-permute-done.3 = f32[120,384]{0,1:T(8,128)S(1)} collective-permute-done((f32[120,384]{0,1:T(8,128)S(1)}, f32[120,384]{0,1:T(8,128)S(1)}, u32[]{:S(2)}, u32[]{:S(2)}) %collective-permute-start.3) | collective-permute-done | bytes 184352 | tf_op jit(solution)/shard_map/ppermute | solution.py:17
  32.1 0.2 copy.11
  32.4 0.6 gather_fusion.1
  33.0 10.1 %fusion.2 = f32[3,120,10,128,1]{3,1,4,2,0:T(8,128)S(1)} fusion(f32[10,3,4,128,128]{4,3,2,1,0:T(8,128)} %param.10, f32[3,4,120,128]{3,2,1,0:T(8,128)S(1)} %bitcast.97, pred[3,4]{1,0:T(4,128)(4,1)S(1)} %get-tuple-element.9), kind=kOutput, calls=%fused_computation.5 | convolution fusion | flops 2831339520 | bytes 10444812 | tf_op jit(solution)/shard_map/kbsij,pbsj->kpbi/dot_general | solution.py:35
  43.1 1.6 fusion.15
  44.9 0.7 fusion.38
  45.5 34.5 %all-reduce = (f32[]{:T(128)}, f32[]{:T(128)}) all-reduce(f32[]{:T(128)} %get-tuple-element.6, f32[]{:T(128)} %get-tuple-element.5), channel_id=1, replica_groups=mesh['group'=2,'node'=16] {'node'}, use_global_device_ids=true, to_apply=%region_1.3 | all-reduce | flops 2 | bytes 16 | tf_op jit(solution)/shard_map/psum | solution.py:45
  81.4 0.7 multiply_reduce_fusion
  82.1 30.1 %psum.30 = f32[]{:T(128)} all-reduce(f32[]{:T(128)} %multiply_reduce_fusion), channel_id=1, replica_groups=mesh['group'=2,'node'=16] {'node'}, use_global_device_ids=true, to_apply=%region_5.7 | all-reduce | flops 1 | bytes 8 | tf_op jit(solution)/shard_map/psum | solution.py:45
  113.6 1.8 %collective-permute-start.4 = (f32[120,384]{0,1:T(8,128)S(1)}, f32[120,384]{0,1:T(8,128)S(1)}, u32[]{:S(2)}, u32[]{:S(2)}) collective-permute-start(f32[120,384]{0,1:T(8,128)S(1)} %multiply_add_fusion.1), channel_id=1, source_target_pairs={{0,1},{1,2},{2,3},{3,4},{4,5},{5,6},{6,7},{7,8},{8,9},{9,10},{10,1... | collective-permute-start | bytes 552968 | tf_op jit(solution)/shard_map/ppermute | solution.py:14
  115.4 1.5 collective-permute-start.5
  116.8 1.8 %collective-permute-done.5 = f32[120,384]{0,1:T(8,128)S(1)} collective-permute-done((f32[120,384]{0,1:T(8,128)S(1)}, f32[120,384]{0,1:T(8,128)S(1)}, u32[]{:S(2)}, u32[]{:S(2)}) %collective-permute-start.5) | collective-permute-done | bytes 184352 | tf_op jit(solution)/shard_map/ppermute | solution.py:17
  119.0 0.6 gather_fusion.2
  119.6 10.1 %fusion = f32[3,120,10,128,1]{3,1,4,2,0:T(8,128)S(1)} fusion(f32[10,3,4,128,128]{4,3,2,1,0:T(8,128)} %param.10, f32[3,4,120,128]{3,2,1,0:T(8,128)S(1)} %bitcast.95, pred[3,4]{1,0:T(4,128)(4,1)S(1)} %get-tuple-element.9), kind=kOutput, calls=%fused_computation.3 | convolution fusion | flops 2831339520 | bytes 10444812 | tf_op jit(solution)/shard_map/kbsij,pbsj->kpbi/dot_general | solution.py:35
  129.7 1.6 fusion.18
  131.5 0.7 fusion.36
  132.3 33.8 %psum.31 = f32[]{:T(128)} all-reduce(f32[]{:T(128)} %fusion.36), channel_id=1, replica_groups=mesh['group'=2,'node'=16] {'node'}, use_global_device_ids=true, to_apply=%region_7.9 | all-reduce | flops 1 | bytes 8 | tf_op jit(solution)/shard_map/psum | solution.py:59
  167.5 0.8 copy.16
  168.3 0.8 copy.17
  (19 shorter events, 1.0 us)
Async XLA Ops:
  0.6 20.4 %copy-start = (f32[10,120,120]{2,1,0:T(8,128)S(1)}, f32[10,120,120]{2,1,0:T(8,128)}, u32[]{:S(2)}) copy-start(f32[10,120,120]{2,1,0:T(8,128)} %param.9) | copy-start | bytes 1728004
  0.6 5.7 %collective-permute-start = (f32[120,384]{1,0:T(8,128)}, f32[120,384]{1,0:T(8,128)S(1)}, u32[]{:S(2)}, u32[]{:S(2)}) collective-permute-start(f32[120,384]{1,0:T(8,128)} %param.8), channel_id=1, source_target_pairs={{0,1},{1,2},{2,3},{3,4},{4,5},{5,6},{6,7},{7,8},{8,9},{9,10},{10,1... | collective-permute-start | bytes 552968 | tf_op jit(solution)/shard_map/ppermute | solution.py:14
  3.2 5.7 %collective-permute-start.1 = (f32[120,384]{1,0:T(8,128)}, f32[120,384]{1,0:T(8,128)S(1)}, u32[]{:S(2)}, u32[]{:S(2)}) collective-permute-start(f32[120,384]{1,0:T(8,128)} %param.8), channel_id=1, source_target_pairs={{1,0},{2,1},{3,2},{4,3},{5,4},{6,5},{7,6},{8,7},{9,8},{10,9},{11,1... | collective-permute-start | bytes 552968 | tf_op jit(solution)/shard_map/ppermute | solution.py:17
  22.8 7.3 %collective-permute-start.2 = (f32[120,384]{0,1:T(8,128)S(1)}, f32[120,384]{0,1:T(8,128)S(1)}, u32[]{:S(2)}, u32[]{:S(2)}) collective-permute-start(f32[120,384]{0,1:T(8,128)S(1)} %bitcast_subtract_fusion), channel_id=1, source_target_pairs={{0,1},{1,2},{2,3},{3,4},{4,5},{5,6},{6,7},{7,8},{8,9},{9,10},{10,1... | collective-permute-start | bytes 552968 | tf_op jit(solution)/shard_map/ppermute | solution.py:14
  28.8 3.3 %collective-permute-start.3 = (f32[120,384]{0,1:T(8,128)S(1)}, f32[120,384]{0,1:T(8,128)S(1)}, u32[]{:S(2)}, u32[]{:S(2)}) collective-permute-start(f32[120,384]{0,1:T(8,128)S(1)} %bitcast_subtract_fusion), channel_id=1, source_target_pairs={{1,0},{2,1},{3,2},{4,3},{5,4},{6,5},{7,6},{8,7},{9,8},{10,9},{11,1... | collective-permute-start | bytes 552968 | tf_op jit(solution)/shard_map/ppermute | solution.py:17
  113.6 3.3 %collective-permute-start.4 = (f32[120,384]{0,1:T(8,128)S(1)}, f32[120,384]{0,1:T(8,128)S(1)}, u32[]{:S(2)}, u32[]{:S(2)}) collective-permute-start(f32[120,384]{0,1:T(8,128)S(1)} %multiply_add_fusion.1), channel_id=1, source_target_pairs={{0,1},{1,2},{2,3},{3,4},{4,5},{5,6},{6,7},{7,8},{8,9},{9,10},{10,1... | collective-permute-start | bytes 552968 | tf_op jit(solution)/shard_map/ppermute | solution.py:14
  115.4 3.3 %collective-permute-start.5 = (f32[120,384]{0,1:T(8,128)S(1)}, f32[120,384]{0,1:T(8,128)S(1)}, u32[]{:S(2)}, u32[]{:S(2)}) collective-permute-start(f32[120,384]{0,1:T(8,128)S(1)} %multiply_add_fusion.1), channel_id=1, source_target_pairs={{1,0},{2,1},{3,2},{4,3},{5,4},{6,5},{7,6},{8,7},{9,8},{10,9},{11,1... | collective-permute-start | bytes 552968 | tf_op jit(solution)/shard_map/ppermute | solution.py:17
  129.7 2.4 %copy-start.1 = (f32[120,384]{1,0:T(8,128)S(1)}, f32[120,384]{1,0:T(8,128)}, u32[]{:S(2)}) copy-start(f32[120,384]{1,0:T(8,128)} %param.8) | copy-start | bytes 552964
where the time goes:
time: 170 us; the launch traced here: 169 us
  blocking collectives  98.4 us (58%)
  matrix products  35.3 us (21%)
  starting transfers between devices  14.3 us (8%)
  waiting for transfers between devices  6.38 us (4%)
  local copies, waits for them, and re-layouts  5.97 us (4%)
  between operations  4.89 us (3%)
  other arithmetic  3.86 us (2%)
    psum x2, blocking collectives, squares(): return lax.psum(jnp.sum(residual * residual), 'node')  64.6 us
    psum x1, blocking collectives, per_device(): step_length = norm_now / lax.psum(jnp.sum(direction * applied), 'node')  33.8 us
    dot_general x3, matrix products, apply_field(): jnp.einsum('kbsij,pbsj->kpbi', stiffness_tiles, picked, precision=lax.Pre...  30.4 us
    ppermute x3, starting transfers between devices, extended(): lax.ppermute(lax.slice_in_dim(block, block.shape[dim] - width, None, axis...  10.2 us
    ppermute x3, waiting for transfers between devices, extended(): lax.ppermute(lax.slice_in_dim(block, 0, width, axis=dim), axis, backward)  6.37 us
    dot_general x3, matrix products, apply_field(): jnp.einsum('kpq,kqbi->pbi', galerkin_mats, mixed_terms, precision=lax.Pre...  4.85 us
    ppermute x3, starting transfers between devices, extended(): lax.ppermute(lax.slice_in_dim(block, 0, width, axis=dim), axis, backward)  4.06 us
  transfers between devices with their start and end apart: 6, of which 3 were waited for; matrix products, arithmetic and copies ran while one was open for 1% of the time, Pallas kernels for 0%

commit v1 on v0

v1 whole, which is shorter than its diff:
```python
import functools

import jax
import jax.numpy as jnp
from jax import lax
from jax.experimental import pallas as pl
from jax.experimental.pallas import tpu as pltpu
from jax.sharding import PartitionSpec as P

MESH = pl.DeviceIdType.MESH
W = 128


def halves(value):
    high = value.astype(jnp.bfloat16)
    low = (value - high.astype(jnp.float32)).astype(jnp.bfloat16)
    return high, low


def first_of(columns, wanted, otherwise):
    found = otherwise
    for slot in range(3, -1, -1):
        found = jnp.where(columns[slot] == wanted, slot, found)
    return found


def kernel(
    n, kl, coefs, cols, rhs, init, gm, tiles, x_out, r_out,
    v_init, v_rhs, v_gm, gpad, gcat, st0, st1, st2, tbf, win, mixed, mbf,
    field, base, sent, got, red_s, red_r, v_x, v_r,
    in_sem, out_sem, halo_send, halo_recv, red_send, red_recv,
):
    me = lax.axis_index("node")
    core = lax.rem(me, 2)
    sibling = me + 1 - 2 * core
    outward = me - 1 + 2 * core
    has_outward = jnp.logical_and(outward >= 0, outward < n)
    edge = pl.multiple_of(core * 2 * W, W)
    staged = (st0, st1, st2)

    loads = [
        pltpu.make_async_copy(init, v_init, in_sem.at[0]),
        pltpu.make_async_copy(tiles.at[:, 0], st0, in_sem.at[1]),
        pltpu.make_async_copy(gm, v_gm, in_sem.at[2]),
        pltpu.make_async_copy(rhs, v_rhs, in_sem.at[3]),
        pltpu.make_async_copy(tiles.at[:, 1], st1, in_sem.at[4]),
        pltpu.make_async_copy(tiles.at[:, 2], st2, in_sem.at[5]),
    ]
    for load in loads:
        load.start()

    barrier = pltpu.get_barrier_semaphore()

    def greet(step, carry):
        peer = lax.rem(me + step, n)
        pl.semaphore_signal(barrier, inc=1, device_id={"node": peer}, device_id_type=MESH)
        return carry

    lax.fori_loop(1, n, greet, 0)

    roles, picks = [], []
    for row in range(3):
        away = [cols[row, slot] - 3 * me - row for slot in range(4)]
        own_first = first_of(away, 0, 0)
        own_last = jnp.int32(0)
        for slot in range(4):
            own_last = jnp.where(away[slot] == 0, slot, own_last)
        left = first_of(away, -1, own_last)
        right = first_of(away, 1, own_last)
        partner = jnp.int32(0)
        for slot in range(4):
            partner = jnp.where(jnp.abs(away[slot]) >= 2, slot, partner)
        order = (own_first, right, left, partner) if row == 0 else (own_first, left, right, partner)
        where = []
        for slot in order:
            rel = cols[row, slot] - 3 * me
            inside = jnp.logical_and(rel >= 0, rel < 3)
            in_pair = rel + 6 * core
            in_pair = jnp.where(in_pair >= 6, 6, in_pair)
            in_pair = jnp.where(in_pair < 0, 6, in_pair)
            in_pair = jnp.where(jnp.logical_and(core == 1, rel == 3), 6, in_pair)
            where.append(jnp.where(inside, rel, in_pair))
        roles.append(order)
        picks.append(where)

    def turned(ref, row):
        part = ref[:, row * W:(row + 1) * W]
        part = jnp.concatenate([part, jnp.zeros((W - coefs, W), jnp.float32)], axis=0)
        return part.T

    def into_window(place, value):
        high, low = halves(value)
        win[place, :, 0:W] = high
        win[place, :, W:2 * W] = low

    loads[0].wait()
    for row in range(3):
        value = turned(v_init, row)
        base[row * W:(row + 1) * W, :] = value
        sent[0, row * W:(row + 1) * W, :] = value
    pl.semaphore_wait(barrier, n - 1)

    def to_sibling(turn):
        return pltpu.make_async_remote_copy(
            src_ref=sent.at[turn], dst_ref=got.at[turn, pl.ds(0, 3 * W)],
            send_sem=halo_send.at[turn, 0], recv_sem=halo_recv.at[turn, 0],
            device_id={"node": sibling}, device_id_type=MESH,
        )

    def to_outward(turn):
        return pltpu.make_async_remote_copy(
            src_ref=sent.at[turn, pl.ds(edge, W)], dst_ref=got.at[turn, pl.ds(3 * W, W)],
            send_sem=halo_send.at[turn, 1], recv_sem=halo_recv.at[turn, 1],
            device_id={"node": outward}, device_id_type=MESH,
        )

    def send(turn):
        @pl.when(has_outward)
        def _():
            to_outward(turn).start()

        to_sibling(turn).start()

    def finish(turn):
        to_sibling(turn).wait()

        @pl.when(has_outward)
        def _():
            to_outward(turn).wait()

    send(0)

    def weights(row, part):
        one = win[picks[row][2 * part]]
        two = win[picks[row][2 * part + 1]]
        return jnp.concatenate([one, two, one, two], axis=0)

    def product(row, part):
        out = jnp.dot(tbf[row, part], weights(row, part), preferred_element_type=jnp.float32)
        return out[:, 0:W] + out[:, W:2 * W]

    def convert(row):
        source = staged[row]

        def body(k, carry):
            at = pl.multiple_of(k * W, W)
            for place in range(4):
                high, low = halves(source[k, roles[row][place]])
                part, side = place // 2, place % 2
                tbf[row, part, pl.ds(at, W), side * W:(side + 1) * W] = high
                tbf[row, part, pl.ds(at, W), (2 + side) * W:(3 + side) * W] = low
            return carry

        lax.fori_loop(0, kl, body, 0)

    def operate(turn, prepare):
        for row in range(3):
            into_window(row, sent[turn, row * W:(row + 1) * W, :])
        for row in range(3):
            if prepare:
                loads[(1, 4, 5)[row]].wait()
                convert(row)
            mixed[row] = product(row, 0)
        finish(turn)
        for place in range(4):
            into_window(3 + place, got[turn, place * W:(place + 1) * W, :])
        for row in range(3):
            high, low = halves(mixed[row] + product(row, 1))
            for k in range(kl):
                mbf[row * W:(row + 1) * W, k * W:(k + 1) * W] = high[k * W:(k + 1) * W]
                mbf[row * W:(row + 1) * W, (kl + k) * W:(kl + k + 1) * W] = low[k * W:(k + 1) * W]
        out = jnp.dot(mbf[...], gcat[...], preferred_element_type=jnp.float32)
        return out[:, 0:W] + out[:, W:2 * W]

    loads[2].wait()
    gpad[...] = jnp.zeros_like(gpad)
    gpad[:, 0:coefs, 0:coefs] = v_gm[...]
    for k in range(kl):
        high, low = halves(gpad[k])
        for copy in range(2):
            at = (copy * kl + k) * W
            gcat[at:at + W, 0:W] = high
            gcat[at:at + W, W:2 * W] = low
    loads[3].wait()
    for row in range(3):
        field[row * W:(row + 1) * W, :] = turned(v_rhs, row)

    def partial(one, two):
        return jnp.sum(one * two, axis=0, keepdims=True)

    def share(turn, parts):
        rows = parts + [jnp.zeros((8 - len(parts), W), jnp.float32)]
        red_s[turn] = jnp.concatenate(rows, axis=0)

        def body(step, carry):
            pltpu.make_async_remote_copy(
                src_ref=red_s.at[turn], dst_ref=red_r.at[turn, step - 1],
                send_sem=red_send.at[turn], recv_sem=red_recv.at[turn],
                device_id={"node": lax.rem(me + step, n)}, device_id_type=MESH,
            ).start()
            return carry

        lax.fori_loop(1, n, body, 0)

    def collect(turn):
        everyone = red_r.at[turn]
        pltpu.make_async_copy(everyone, everyone, red_recv.at[turn]).wait()
        total = red_s[turn] + jnp.sum(red_r[turn], axis=0)
        return jnp.sum(total, axis=1, keepdims=True)

    r0 = field[...] - operate(0, True)
    sent[1] = r0
    send(1)
    w = operate(1, False)
    sent[2] = w
    send(2)
    r0 = sent[1]
    share(0, [partial(r0, r0), partial(r0, w)])
    z = operate(2, False)
    sums = collect(0)
    rr, rw = sums[0:1], sums[1:2]
    step0 = rr / rw
    r0, w = sent[1], sent[2]
    r1 = r0 - step0 * w
    q = w - step0 * z
    share(1, [partial(r1, r1), partial(r1, q), partial(r0, q) + partial(r1, w)])
    x1 = base[...] + step0 * r0
    sums = collect(1)
    new = sums[0:1]
    beta = new / rr
    step1 = new / (sums[1:2] + beta * (sums[2:3] + beta * rw))
    x2 = x1 + step1 * (r1 + beta * r0)
    r2 = r1 - step1 * (q + beta * w)
    for row in range(3):
        v_x[:, row * W:(row + 1) * W] = x2[row * W:(row + 1) * W].T[0:coefs]
        v_r[:, row * W:(row + 1) * W] = r2[row * W:(row + 1) * W].T[0:coefs]
    stores = [
        pltpu.make_async_copy(v_x, x_out, out_sem.at[0]),
        pltpu.make_async_copy(v_r, r_out, out_sem.at[1]),
    ]
    for store in stores:
        store.start()
    for turn in range(2):
        everyone = red_r.at[turn]
        pltpu.make_async_copy(everyone, everyone, red_send.at[turn]).wait()
    for store in stores:
        store.wait()


def per_device(right_side, initial, galerkin_mats, stiffness_tiles, block_cols):
    n = lax.axis_size("node")
    coefs, nodes = right_side.shape
    kl = galerkin_mats.shape[0]
    assert stiffness_tiles.shape[1:] == (3, 4, W, W) and coefs <= W and n % 2 == 0
    f32, b16 = jnp.float32, jnp.bfloat16
    anywhere = pl.BlockSpec(memory_space=pl.ANY)
    out = jax.ShapeDtypeStruct(right_side.shape, f32)
    staged = pltpu.VMEM((kl, 4, W, W), f32)
    return pl.pallas_call(
        functools.partial(kernel, n, kl, coefs),
        out_shape=(out, out),
        in_specs=[pl.BlockSpec(memory_space=pltpu.SMEM)] + [anywhere] * 4,
        out_specs=(anywhere, anywhere),
        scratch_shapes=[
            pltpu.VMEM((coefs, nodes), f32),
            pltpu.VMEM((coefs, nodes), f32),
            pltpu.VMEM(galerkin_mats.shape, f32),
            pltpu.VMEM((kl, W, W), f32),
            pltpu.VMEM((2 * kl * W, 2 * W), b16),
            staged, staged, staged,
            pltpu.VMEM((3, 2, kl * W, 4 * W), b16),
            pltpu.VMEM((7, W, 2 * W), b16),
            pltpu.VMEM((3, kl * W, W), f32),
            pltpu.VMEM((3 * W, 2 * kl * W), b16),
            pltpu.VMEM((3 * W, W), f32),
            pltpu.VMEM((3 * W, W), f32),
            pltpu.VMEM((3, 3 * W, W), f32),
            pltpu.VMEM((3, 4 * W, W), f32),
            pltpu.VMEM((2, 8, W), f32),
            pltpu.VMEM((2, n - 1, 8, W), f32),
            pltpu.VMEM((coefs, nodes), f32),
            pltpu.VMEM((coefs, nodes), f32),
            pltpu.SemaphoreType.DMA((6,)),
            pltpu.SemaphoreType.DMA((2,)),
            pltpu.SemaphoreType.DMA((3, 2)),
            pltpu.SemaphoreType.DMA((3, 2)),
            pltpu.SemaphoreType.DMA((2,)),
            pltpu.SemaphoreType.DMA((2,)),
        ],
        compiler_params=pltpu.CompilerParams(
            collective_id=0, has_side_effects=True, vmem_limit_bytes=56 * 2**20
        ),
    )(block_cols, right_side, initial, galerkin_mats, stiffness_tiles)


def solution(mesh):
    placed = (
        P(None, ("group", "node")),
        P(None, ("group", "node")),
        P(),
        P(None, ("group", "node"), None, None, None),
        P(("group", "node"), None),
    )
    return jax.shard_map(
        per_device,
        mesh=mesh,
        in_specs=placed,
        out_specs=(P(None, ("group", "node")), P(None, ("group", "node"))),
        check_vma=False,
    )
```

time: 170 us -> 33.7 us (0.20)
  blocking collectives: 98.4 us -> 0 us
  matrix products: 35.3 us -> 0 us
  Pallas kernels: 0 us -> 29.6 us
  starting transfers between devices: 14.3 us -> 0 us
  waiting for transfers between devices: 6.38 us -> 0 us
  between operations: 4.89 us -> 0.64 us
  other arithmetic: 3.86 us -> 0 us
  local copies, waits for them, and re-layouts: 5.97 us -> 3.22 us
    psum x3 -> x0, blocking collectives: 98.4 us -> none  [the longest x2 64.6 us: squares(): return lax.psum(jnp.sum(residual * residual), 'node')]
    dot_general x6 -> x0, matrix products: 35.3 us -> none  [the longest x3 30.4 us: apply_field(): jnp.einsum('kbsij,pbsj->kpbi', stiffness_tiles, picked, precision=lax.Pre...]
    pallas_call x0 -> x1, Pallas kernels: none -> 29.6 us  [per_device(): pl.pallas_call(functools.partial(kernel, n, kl, coefs), out_shape=(out, o...]
    ppermute x6 -> x0, starting transfers between devices: 14.3 us -> none  [the longest x3 10.2 us: extended(): lax.ppermute(lax.slice_in_dim(block, block.shape[dim] - width, None, axis...]
    ppermute x6 -> x0, waiting for transfers between devices: 6.38 us -> none  [the longest x3 6.37 us: extended(): lax.ppermute(lax.slice_in_dim(block, 0, width, axis=dim), axis, backward)]
    reduce_sum x3 -> x0, other arithmetic: 1.99 us -> none  [the longest x2 1.33 us: per_device(): step_length = norm_now / lax.psum(jnp.sum(direction * applied), 'node')]
    gather x3 -> x0, local copies, waits for them, and re-layouts: 1.81 us -> none  [apply_field(): picked = jnp.take(blocks, local_index, axis=1)]
  transfers between devices with their start and end apart: 6 -> 0, of which waited for: 3 -> 0; matrix products, arithmetic and copies ran while one was open for 1% -> 0% of each run, Pallas kernels for 0% -> 0%
where the time goes in v1:
time: 33.7 us; the launch traced here: 33.5 us
  Pallas kernels  29.6 us (88%)
  local copies, waits for them, and re-layouts  3.22 us (10%)
  between operations  0.64 us (2%)
    pallas_call x1, Pallas kernels, per_device(): pl.pallas_call(functools.partial(kernel, n, kl, coefs), out_shape=(out, o...  29.6 us
    unnamed x2, local copies, waits for them, and re-layouts  3.22 us

profile of v1, /device:TPU:0, one launch (start us, length us, event | category | flops | bytes accessed | tf_op | source)
XLA Modules:
  0.0 33.5 jit_solution(239244622192511904)
XLA Ops:
  0.6 29.6 %shard_map.68 = (f32[120,384]{1,0:T(8,128)}, f32[120,384]{1,0:T(8,128)}) custom-call(s32[3,4]{1,0:T(4,128)} %cols.1, f32[120,384]{1,0:T(8,128)} %rhs.1, f32[120,384]{1,0:T(8,128)} %init.1, f32[10,120,120]{2,1,0:T(8,128)} %gm.1, f32[10,3,4,128,128]{4,3,2,1,0:T(8,128)} %tiles.1), custom_call_target="tpu_custom_call" | custom-call | tf_op jit(solution)/shard_map/pallas_call | solution.py:259
  30.3 1.6 %copy.9 = f32[120,384]{1,0:T(8,128)} copy(f32[120,384]{1,0:T(8,128)} %get-tuple-element.4) | data formatting | bytes 368640
  31.9 1.6 %copy.10 = f32[120,384]{1,0:T(8,128)} copy(f32[120,384]{1,0:T(8,128)} %get-tuple-element.5) | data formatting | bytes 368640

commit v2 on v1

v2 whole, which is shorter than its diff:
```python
import functools

import jax
import jax.numpy as jnp
from jax import lax
from jax.experimental import pallas as pl
from jax.experimental.pallas import tpu as pltpu
from jax.sharding import PartitionSpec as P

MESH = pl.DeviceIdType.MESH
W = 128


def halves(value):
    high = value.astype(jnp.bfloat16)
    low = (value - high.astype(jnp.float32)).astype(jnp.bfloat16)
    return high, low


def first_of(columns, wanted, otherwise):
    found = otherwise
    for slot in range(3, -1, -1):
        found = jnp.where(columns[slot] == wanted, slot, found)
    return found


def kernel(
    n, kl, coefs, cols, rhs, init, gm, tiles, out,
    v_init, v_rhs, v_gm, gpad, gcat, st0, st1, st2, tbf, win, mixed, mbf,
    vec, base, sent, got, red_s, red_r, pair_r,
    in_sem, halo_send, halo_recv, red_send, red_recv, pair_send, pair_recv,
):
    me = lax.axis_index("node")
    core = lax.rem(me, 2)
    sibling = me + 1 - 2 * core
    outward = me - 1 + 2 * core
    has_outward = jnp.logical_and(outward >= 0, outward < n)
    rows = [2 * core, 1, 2 - 2 * core]
    lanes = [pl.ds(pl.multiple_of(row * W, W), W) for row in rows]
    staged = (st0, st1, st2)

    loads = [
        pltpu.make_async_copy(init, v_init, in_sem.at[0]),
        pltpu.make_async_copy(tiles.at[:, rows[0]], st0, in_sem.at[1]),
        pltpu.make_async_copy(gm, v_gm, in_sem.at[2]),
        pltpu.make_async_copy(rhs, v_rhs, in_sem.at[3]),
        pltpu.make_async_copy(tiles.at[:, rows[1]], st1, in_sem.at[4]),
        pltpu.make_async_copy(tiles.at[:, rows[2]], st2, in_sem.at[5]),
    ]
    for load in loads:
        load.start()

    barrier = pltpu.get_barrier_semaphore()

    def greet(peer):
        pl.semaphore_signal(barrier, inc=1, device_id={"node": peer}, device_id_type=MESH)

    greet(sibling)

    @pl.when(has_outward)
    def _():
        greet(outward)

    def greet_same_core(step, carry):
        greet(lax.rem(me + 2 * step, n))
        return carry

    lax.fori_loop(1, n // 2, greet_same_core, 0)

    roles, picks = [], []
    for i in range(3):
        spots = []
        for slot in range(4):
            rel = cols[rows[i], slot] - 3 * me
            spots.append(jnp.where(core == 1, 2 - rel, rel))
        away = [spot - i for spot in spots]
        own_first = first_of(away, 0, 0)
        own_last = jnp.int32(0)
        partner = jnp.int32(0)
        for slot in range(4):
            own_last = jnp.where(away[slot] == 0, slot, own_last)
            partner = jnp.where(jnp.abs(away[slot]) >= 2, slot, partner)
        out_side = first_of(away, -1, own_last)
        in_side = first_of(away, 1, own_last)
        if i == 0:
            order = (own_first, in_side, out_side, partner)
        else:
            order = (own_first, out_side, in_side, partner)
        where = []
        for slot in order:
            spot = jnp.int32(0)
            for other in range(4):
                spot = jnp.where(slot == other, spots[other], spot)
            where.append(jnp.where(spot < 0, 6, jnp.where(spot > 2, jnp.maximum(8 - spot, 0), spot)))
        roles.append(order)
        picks.append(where)

    def turned(ref, i):
        part = ref[:, lanes[i]]
        part = jnp.concatenate([part, jnp.zeros((W - coefs, W), jnp.float32)], axis=0)
        return part.T

    def into_window(place, value):
        high, low = halves(value)
        win[place, :, 0:W] = high
        win[place, :, W:2 * W] = low

    def block_copy(turn, i, peer, place):
        return pltpu.make_async_remote_copy(
            src_ref=sent.at[turn, i], dst_ref=got.at[turn, place],
            send_sem=halo_send.at[turn, place], recv_sem=halo_recv.at[turn, place],
            device_id={"node": peer}, device_id_type=MESH,
        )

    def send(turn, i):
        if i == 0:
            @pl.when(has_outward)
            def _():
                block_copy(turn, 0, outward, 3).start()

        block_copy(turn, i, sibling, i).start()

    def finish(turn):
        for i in range(3):
            block_copy(turn, i, sibling, i).wait()

        @pl.when(has_outward)
        def _():
            block_copy(turn, 0, outward, 3).wait()

        for place in range(4):
            into_window(3 + place, got[turn, place])

    loads[0].wait()
    for i in range(3):
        value = turned(v_init, i)
        base[i] = value
        sent[0, i] = value
    pl.semaphore_wait(barrier, n // 2 + has_outward.astype(jnp.int32))
    for i in range(3):
        send(0, i)

    def product(i, part):
        one = win[picks[i][2 * part]]
        two = win[picks[i][2 * part + 1]]
        sides = jnp.concatenate([one, two, one, two], axis=0)
        made = jnp.dot(tbf[i, part], sides, preferred_element_type=jnp.float32)
        return made[:, 0:W] + made[:, W:2 * W]

    def convert(i):
        source = staged[i]

        def body(k, carry):
            at = pl.multiple_of(k * W, W)
            for place in range(4):
                high, low = halves(source[k, roles[i][place]])
                part, side = place // 2, place % 2
                tbf[i, part, pl.ds(at, W), side * W:(side + 1) * W] = high
                tbf[i, part, pl.ds(at, W), (2 + side) * W:(3 + side) * W] = low
            return carry

        lax.fori_loop(0, kl, body, 0)

    def operate(turn, prepare, use, between=None):
        for i in range(3):
            into_window(i, sent[turn, i])
        for i in range(3):
            if prepare:
                loads[(1, 4, 5)[i]].wait()
                convert(i)
            mixed[i] = product(i, 0)
        if between is not None:
            between()
        finish(turn)
        for i in range(3):
            high, low = halves(mixed[i] + product(i, 1))
            for k in range(kl):
                mbf[i, 0:W, k * W:(k + 1) * W] = high[k * W:(k + 1) * W]
                mbf[i, W:2 * W, k * W:(k + 1) * W] = low[k * W:(k + 1) * W]
            made = jnp.dot(mbf[i], gcat[...], preferred_element_type=jnp.float32)
            made = made[0:W] + made[W:2 * W]
            use(i, made[:, 0:W] + made[:, W:2 * W])

    loads[2].wait()
    gpad[...] = jnp.zeros_like(gpad)
    gpad[:, 0:coefs, 0:coefs] = v_gm[...]
    for k in range(kl):
        high, low = halves(gpad[k])
        gcat[k * W:(k + 1) * W, 0:W] = high
        gcat[k * W:(k + 1) * W, W:2 * W] = low
    loads[3].wait()
    for i in range(3):
        vec[0, i] = turned(v_rhs, i)

    def partial(pairs):
        return sum(jnp.sum(one * two, axis=0, keepdims=True) for one, two in pairs)

    def pair_copy(turn):
        return pltpu.make_async_remote_copy(
            src_ref=red_s.at[turn, 0], dst_ref=pair_r.at[turn],
            send_sem=pair_send.at[turn], recv_sem=pair_recv.at[turn],
            device_id={"node": sibling}, device_id_type=MESH,
        )

    def share(turn, parts):
        parts = parts + [jnp.zeros((8 - len(parts), W), jnp.float32)]
        red_s[turn, 0] = jnp.concatenate(parts, axis=0)
        pair_copy(turn).start()

    def spread(turn):
        pair_copy(turn).wait()
        red_s[turn, 1] = red_s[turn, 0] + pair_r[turn]

        def body(step, carry):
            pltpu.make_async_remote_copy(
                src_ref=red_s.at[turn, 1], dst_ref=red_r.at[turn, step - 1],
                send_sem=red_send.at[turn], recv_sem=red_recv.at[turn],
                device_id={"node": lax.rem(me + 2 * step, n)}, device_id_type=MESH,
            ).start()
            return carry

        lax.fori_loop(1, n // 2, body, 0)

    def collect(turn):
        everyone = red_r.at[turn]
        pltpu.make_async_copy(everyone, everyone, red_recv.at[turn]).wait()
        total = red_s[turn, 1] + jnp.sum(red_r[turn], axis=0)
        return jnp.sum(total, axis=1, keepdims=True)

    three = range(3)

    def first(i, applied):
        vec[1, i] = applied
        sent[1, i] = vec[0, i] - applied
        send(1, i)

    operate(0, True, first)
    share(0, [
        partial([(base[i], base[i]) for i in three]),
        partial([(base[i], vec[1, i]) for i in three]),
    ])

    guess = []

    def second(i, applied):
        vec[0, i] = applied
        if i == 0:
            sums = collect(0)
            usable = sums[1:2] > 1e-6 * sums[0:1]
            ratio = sums[0:1] / jnp.where(usable, sums[1:2], 1.0)
            usable = jnp.logical_and(usable, ratio > 1e-6)
            guess.append(jnp.where(usable, 1.0, 0.0))
            guess.append(jnp.where(usable, -ratio, 1.0))
        sent[2, i] = guess[0] * sent[1, i] + guess[1] * applied
        send(2, i)

    operate(1, False, second, lambda: spread(0))
    share(1, [
        partial([(sent[1, i], sent[1, i]) for i in three]),
        partial([(sent[1, i], vec[0, i]) for i in three]),
    ])

    def third(i, applied):
        vec[1, i] = applied

    operate(2, False, third, lambda: spread(1))
    sums = collect(1)
    rr, rw = sums[0:1], sums[1:2]
    step0 = rr / rw
    scaled = step0 / guess[1]
    r0 = [sent[1, i] for i in three]
    w = [vec[0, i] for i in three]
    r1 = [r0[i] - step0 * w[i] for i in three]
    q = [(1.0 + scaled * guess[0]) * w[i] - scaled * vec[1, i] for i in three]
    share(2, [
        partial(list(zip(r1, r1))),
        partial(list(zip(r1, q))),
        partial(list(zip(r0, q)) + list(zip(r1, w))),
    ])
    spread(2)
    x1 = [base[i] + step0 * r0[i] for i in three]
    sums = collect(2)
    new = sums[0:1]
    beta = new / rr
    step1 = new / (sums[1:2] + beta * (sums[2:3] + beta * rw))
    for i in three:
        x2 = x1[i] + step1 * (r1[i] + beta * r0[i])
        r2 = r1[i] - step1 * (q[i] + beta * w[i])
        out[0, :, lanes[i]] = x2.T[0:coefs]
        out[1, :, lanes[i]] = r2.T[0:coefs]
    for turn in range(3):
        everyone = red_r.at[turn]
        pltpu.make_async_copy(everyone, everyone, red_send.at[turn]).wait()


def unstack(both, x_out, r_out):
    x_out[...] = both[0]
    r_out[...] = both[1]


def per_device(right_side, initial, galerkin_mats, stiffness_tiles, block_cols):
    n = lax.axis_size("node")
    coefs, nodes = right_side.shape
    kl = galerkin_mats.shape[0]
    assert stiffness_tiles.shape[1:] == (3, 4, W, W) and coefs <= W and n % 2 == 0
    f32, b16 = jnp.float32, jnp.bfloat16
    anywhere = pl.BlockSpec(memory_space=pl.ANY)
    vmem = pl.BlockSpec(memory_space=pltpu.VMEM)
    staged = pltpu.VMEM((kl, 4, W, W), f32)
    both = pl.pallas_call(
        functools.partial(kernel, n, kl, coefs),
        out_shape=jax.ShapeDtypeStruct((2, coefs, nodes), f32),
        in_specs=[pl.BlockSpec(memory_space=pltpu.SMEM)] + [anywhere] * 4,
        out_specs=vmem,
        scratch_shapes=[
            pltpu.VMEM((coefs, nodes), f32),
            pltpu.VMEM((coefs, nodes), f32),
            pltpu.VMEM(galerkin_mats.shape, f32),
            pltpu.VMEM((kl, W, W), f32),
            pltpu.VMEM((kl * W, 2 * W), b16),
            staged, staged, staged,
            pltpu.VMEM((3, 2, kl * W, 4 * W), b16),
            pltpu.VMEM((7, W, 2 * W), b16),
            pltpu.VMEM((3, kl * W, W), f32),
            pltpu.VMEM((3, 2 * W, kl * W), b16),
            pltpu.VMEM((2, 3, W, W), f32),
            pltpu.VMEM((3, W, W), f32),
            pltpu.VMEM((3, 3, W, W), f32),
            pltpu.VMEM((3, 4, W, W), f32),
            pltpu.VMEM((3, 2, 8, W), f32),
            pltpu.VMEM((3, n // 2 - 1, 8, W), f32),
            pltpu.VMEM((3, 8, W), f32),
            pltpu.SemaphoreType.DMA((6,)),
            pltpu.SemaphoreType.DMA((3, 4)),
            pltpu.SemaphoreType.DMA((3, 4)),
            pltpu.SemaphoreType.DMA((3,)),
            pltpu.SemaphoreType.DMA((3,)),
            pltpu.SemaphoreType.DMA((3,)),
            pltpu.SemaphoreType.DMA((3,)),
        ],
        compiler_params=pltpu.CompilerParams(
            collective_id=0, has_side_effects=True, vmem_limit_bytes=56 * 2**20
        ),
    )(block_cols, right_side, initial, galerkin_mats, stiffness_tiles)
    one = jax.ShapeDtypeStruct((coefs, nodes), f32)
    return pl.pallas_call(
        unstack, out_shape=(one, one), in_specs=[vmem], out_specs=(vmem, vmem)
    )(both)


def solution(mesh):
    placed = (
        P(None, ("group", "node")),
        P(None, ("group", "node")),
        P(),
        P(None, ("group", "node"), None, None, None),
        P(("group", "node"), None),
    )
    return jax.shard_map(
        per_device,
        mesh=mesh,
        in_specs=placed,
        out_specs=(P(None, ("group", "node")), P(None, ("group", "node"))),
        check_vma=False,
    )
```

time: 33.7 us -> 36.1 us (1.071)
  Pallas kernels: 29.6 us -> 35.3 us
  local copies, waits for them, and re-layouts: 3.22 us -> 0 us
    pallas_call x1 -> x2, Pallas kernels: 29.6 us -> 35.3 us  [the longest x1 33.6 us: per_device(): pl.pallas_call(functools.partial(kernel, n, kl, coefs), out_shape=jax.Sha...]
    unnamed x2 -> x0, local copies, waits for them, and re-layouts: 3.22 us -> none
where the time goes in v2:
time: 36.1 us; the launch traced here: 35.9 us
  Pallas kernels  35.3 us (98%)
  between operations  0.64 us (2%)
    pallas_call x1, Pallas kernels, per_device(): pl.pallas_call(functools.partial(kernel, n, kl, coefs), out_shape=jax.Sha...  33.6 us
    pallas_call x1, Pallas kernels, per_device(): pl.pallas_call(unstack, out_shape=(one, one), in_specs=[vmem], out_specs=...  1.74 us

profile of v2, /device:TPU:0, one launch (start us, length us, event | category | flops | bytes accessed | tf_op | source)
XLA Modules:
  0.0 35.9 jit_solution(7326876614840428316)
XLA Ops:
  0.6 33.6 %shard_map.68.both = f32[2,120,384]{2,1,0:T(8,128)} custom-call(s32[3,4]{1,0:T(4,128)} %cols.1, f32[120,384]{1,0:T(8,128)} %rhs.1, f32[120,384]{1,0:T(8,128)} %init.1, f32[10,120,120]{2,1,0:T(8,128)} %gm.1, f32[10,3,4,128,128]{4,3,2,1,0:T(8,128)} %tiles.1), custom_call_target="tpu_custom_call" | custom-call | tf_op jit(solution)/shard_map/pallas_call | solution.py:310
  34.2 1.7 %shard_map.69 = (f32[120,384]{1,0:T(8,128)}, f32[120,384]{1,0:T(8,128)}) custom-call(f32[2,120,384]{2,1,0:T(8,128)} %shard_map.68.both), custom_call_target="tpu_custom_call" | custom-call | tf_op jit(solution)/shard_map/pallas_call | solution.py:346

commit v3 on v2

--- a/solution.py
+++ b/solution.py
@@ -27,8 +27,8 @@
 def kernel(
     n, kl, coefs, cols, rhs, init, gm, tiles, out,
     v_init, v_rhs, v_gm, gpad, gcat, st0, st1, st2, tbf, win, mixed, mbf,
-    vec, base, sent, got, red_s, red_r, pair_r,
-    in_sem, halo_send, halo_recv, red_send, red_recv, pair_send, pair_recv,
+    vec, base, sent, got, red_s, red_r,
+    in_sem, halo_send, halo_recv, red_send, red_recv,
 ):
     me = lax.axis_index("node")
     core = lax.rem(me, 2)
@@ -55,17 +55,11 @@
     def greet(peer):
         pl.semaphore_signal(barrier, inc=1, device_id={"node": peer}, device_id_type=MESH)
 
-    greet(sibling)
-
-    @pl.when(has_outward)
-    def _():
-        greet(outward)
-
-    def greet_same_core(step, carry):
-        greet(lax.rem(me + 2 * step, n))
+    def greet_all(step, carry):
+        greet(lax.rem(me + step, n))
         return carry
 
-    lax.fori_loop(1, n // 2, greet_same_core, 0)
+    lax.fori_loop(1, n, greet_all, 0)
 
     roles, picks = [], []
     for i in range(3):
@@ -136,7 +130,7 @@
         value = turned(v_init, i)
         base[i] = value
         sent[0, i] = value
-    pl.semaphore_wait(barrier, n // 2 + has_outward.astype(jnp.int32))
+    pl.semaphore_wait(barrier, n - 1)
     for i in range(3):
         send(0, i)
 
@@ -161,7 +155,7 @@
 
         lax.fori_loop(0, kl, body, 0)
 
-    def operate(turn, prepare, use, between=None):
+    def operate(turn, prepare, use):
         for i in range(3):
             into_window(i, sent[turn, i])
         for i in range(3):
@@ -169,8 +163,6 @@
                 loads[(1, 4, 5)[i]].wait()
                 convert(i)
             mixed[i] = product(i, 0)
-        if between is not None:
-            between()
         finish(turn)
         for i in range(3):
             high, low = halves(mixed[i] + product(i, 1))
@@ -195,36 +187,24 @@
     def partial(pairs):
         return sum(jnp.sum(one * two, axis=0, keepdims=True) for one, two in pairs)
 
-    def pair_copy(turn):
-        return pltpu.make_async_remote_copy(
-            src_ref=red_s.at[turn, 0], dst_ref=pair_r.at[turn],
-            send_sem=pair_send.at[turn], recv_sem=pair_recv.at[turn],
-            device_id={"node": sibling}, device_id_type=MESH,
-        )
-
     def share(turn, parts):
         parts = parts + [jnp.zeros((8 - len(parts), W), jnp.float32)]
-        red_s[turn, 0] = jnp.concatenate(parts, axis=0)
-        pair_copy(turn).start()
-
-    def spread(turn):
-        pair_copy(turn).wait()
-        red_s[turn, 1] = red_s[turn, 0] + pair_r[turn]
+        red_s[turn] = jnp.concatenate(parts, axis=0)
 
         def body(step, carry):
             pltpu.make_async_remote_copy(
-                src_ref=red_s.at[turn, 1], dst_ref=red_r.at[turn, step - 1],
+                src_ref=red_s.at[turn], dst_ref=red_r.at[turn, step - 1],
                 send_sem=red_send.at[turn], recv_sem=red_recv.at[turn],
-                device_id={"node": lax.rem(me + 2 * step, n)}, device_id_type=MESH,
+                device_id={"node": lax.rem(me + step, n)}, device_id_type=MESH,
             ).start()
             return carry
 
-        lax.fori_loop(1, n // 2, body, 0)
+        lax.fori_loop(1, n, body, 0)
 
     def collect(turn):
         everyone = red_r.at[turn]
         pltpu.make_async_copy(everyone, everyone, red_recv.at[turn]).wait()
-        total = red_s[turn, 1] + jnp.sum(red_r[turn], axis=0)
+        total = red_s[turn] + jnp.sum(red_r[turn], axis=0)
         return jnp.sum(total, axis=1, keepdims=True)
 
     three = range(3)
@@ -254,7 +234,7 @@
         sent[2, i] = guess[0] * sent[1, i] + guess[1] * applied
         send(2, i)
 
-    operate(1, False, second, lambda: spread(0))
+    operate(1, False, second)
     share(1, [
         partial([(sent[1, i], sent[1, i]) for i in three]),
         partial([(sent[1, i], vec[0, i]) for i in three]),
@@ -263,7 +243,7 @@
     def third(i, applied):
         vec[1, i] = applied
 
-    operate(2, False, third, lambda: spread(1))
+    operate(2, False, third)
     sums = collect(1)
     rr, rw = sums[0:1], sums[1:2]
     step0 = rr / rw
@@ -277,7 +257,6 @@
         partial(list(zip(r1, q))),
         partial(list(zip(r0, q)) + list(zip(r1, w))),
     ])
-    spread(2)
     x1 = [base[i] + step0 * r0[i] for i in three]
     sums = collect(2)
     new = sums[0:1]
@@ -327,14 +306,11 @@
             pltpu.VMEM((3, W, W), f32),
             pltpu.VMEM((3, 3, W, W), f32),
             pltpu.VMEM((3, 4, W, W), f32),
-            pltpu.VMEM((3, 2, 8, W), f32),
-            pltpu.VMEM((3, n // 2 - 1, 8, W), f32),
             pltpu.VMEM((3, 8, W), f32),
+            pltpu.VMEM((3, n - 1, 8, W), f32),
             pltpu.SemaphoreType.DMA((6,)),
             pltpu.SemaphoreType.DMA((3, 4)),
             pltpu.SemaphoreType.DMA((3, 4)),
-            pltpu.SemaphoreType.DMA((3,)),
-            pltpu.SemaphoreType.DMA((3,)),
             pltpu.SemaphoreType.DMA((3,)),
             pltpu.SemaphoreType.DMA((3,)),
         ],

time: 36.1 us -> 33.4 us (0.925)
  Pallas kernels: 35.3 us -> 32.6 us
    pallas_call x1, Pallas kernels: 33.6 us -> 30.9 us  [per_device(): pl.pallas_call(functools.partial(kernel, n, kl, coefs), out_shape=jax.Sha...]
where the time goes in v3:
time: 33.4 us; the launch traced here: 33.3 us
  Pallas kernels  32.6 us (98%)
  between operations  0.64 us (2%)
    pallas_call x1, Pallas kernels, per_device(): pl.pallas_call(functools.partial(kernel, n, kl, coefs), out_shape=jax.Sha...  30.9 us
    pallas_call x1, Pallas kernels, per_device(): pl.pallas_call(unstack, out_shape=(one, one), in_specs=[vmem], out_specs=...  1.74 us

profile of v3, /device:TPU:0, one launch (start us, length us, event | category | flops | bytes accessed | tf_op | source)
XLA Modules:
  0.0 33.3 jit_solution(4692731330868952079)
XLA Ops:
  0.6 30.9 %shard_map.68.both = f32[2,120,384]{2,1,0:T(8,128)} custom-call(s32[3,4]{1,0:T(4,128)} %cols.1, f32[120,384]{1,0:T(8,128)} %rhs.1, f32[120,384]{1,0:T(8,128)} %init.1, f32[10,120,120]{2,1,0:T(8,128)} %gm.1, f32[10,3,4,128,128]{4,3,2,1,0:T(8,128)} %tiles.1), custom_call_target="tpu_custom_call" | custom-call | tf_op jit(solution)/shard_map/pallas_call | solution.py:289
  31.5 1.7 %shard_map.69 = (f32[120,384]{1,0:T(8,128)}, f32[120,384]{1,0:T(8,128)}) custom-call(f32[2,120,384]{2,1,0:T(8,128)} %shard_map.68.both), custom_call_target="tpu_custom_call" | custom-call | tf_op jit(solution)/shard_map/pallas_call | solution.py:322

commit v4 on v3

--- a/solution.py
+++ b/solution.py
@@ -210,16 +210,12 @@
     three = range(3)
 
     def first(i, applied):
-        vec[1, i] = applied
         sent[1, i] = vec[0, i] - applied
         send(1, i)
+        if i == 0:
+            share(0, [partial([(base[0], base[0])]), partial([(base[0], applied)])])
 
     operate(0, True, first)
-    share(0, [
-        partial([(base[i], base[i]) for i in three]),
-        partial([(base[i], vec[1, i]) for i in three]),
-    ])
-
     guess = []
 
     def second(i, applied):

time: 33.4 us -> 31.8 us (0.952)
  Pallas kernels: 32.6 us -> 31 us
    pallas_call x1, Pallas kernels: 30.9 us -> 29.2 us  [per_device(): pl.pallas_call(functools.partial(kernel, n, kl, coefs), out_shape=jax.Sha...]
where the time goes in v4:
time: 31.8 us; the launch traced here: 31.6 us
  Pallas kernels  31 us (97%)
  between operations  0.64 us (2%)
    pallas_call x1, Pallas kernels, per_device(): pl.pallas_call(functools.partial(kernel, n, kl, coefs), out_shape=jax.Sha...  29.2 us
    pallas_call x1, Pallas kernels, per_device(): pl.pallas_call(unstack, out_shape=(one, one), in_specs=[vmem], out_specs=...  1.74 us

profile of v4, /device:TPU:0, one launch (start us, length us, event | category | flops | bytes accessed | tf_op | source)
XLA Modules:
  0.0 31.6 jit_solution(18285867930581482387)
XLA Ops:
  0.6 29.2 %shard_map.68.both = f32[2,120,384]{2,1,0:T(8,128)} custom-call(s32[3,4]{1,0:T(4,128)} %cols.1, f32[120,384]{1,0:T(8,128)} %rhs.1, f32[120,384]{1,0:T(8,128)} %init.1, f32[10,120,120]{2,1,0:T(8,128)} %gm.1, f32[10,3,4,128,128]{4,3,2,1,0:T(8,128)} %tiles.1), custom_call_target="tpu_custom_call" | custom-call | tf_op jit(solution)/shard_map/pallas_call | solution.py:285
  29.9 1.7 %shard_map.69 = (f32[120,384]{1,0:T(8,128)}, f32[120,384]{1,0:T(8,128)}) custom-call(f32[2,120,384]{2,1,0:T(8,128)} %shard_map.68.both), custom_call_target="tpu_custom_call" | custom-call | tf_op jit(solution)/shard_map/pallas_call | solution.py:318
